TPU v7x, 128 devices: a whole 4x4x4 slice. The times are simulated.
128 devices in a mesh: pp: 2 (over core), fsdp: 16 (over y, x), tp: 4 (over z).
Axes of the slice: x: 4, y: 4, z: 4, core: 2. Of those that a mesh axis runs over, the one named last changes fastest.
Arguments:
- inputs: bfloat16 [2, 512, 8192], P(None, 'tp', 'fsdp'), may hold values from -12 to 12
- head_grad: bfloat16 [2, 512, 8192], P(None, 'tp', 'fsdp'), may hold values from -0.3 to 0.3
- noise_mask: int32 [2, 512], P(None, 'tp'), may hold values 0 or 1
- lengths: int32 [2, 16, 2], replicated, may hold values from 1 to 24, 32 in all within a row
- rewards: int32 [2, 16, 2], replicated, may hold values from 0 to 3
- groups: int32 [2, 16, 2], replicated, may hold values from 0 to 31, as said below
- query_weight: bfloat16 [2, 8192, 4096], P('pp', 'fsdp', 'tp'), may hold values from -0.0625 to 0.0625
- key_weight: bfloat16 [2, 8192, 1024], P('pp', 'fsdp', 'tp'), may hold values from -0.0625 to 0.0625
- value_weight: bfloat16 [2, 8192, 1024], P('pp', 'fsdp', 'tp'), may hold values from -1 to 1
- out_weight: bfloat16 [2, 4096, 8192], P('pp', 'tp', 'fsdp'), may hold values from -1 to 1
Outputs:
- query_weight_grad: float32 [2, 8192, 4096], P('pp', 'fsdp', 'tp')
- key_weight_grad: float32 [2, 8192, 1024], P('pp', 'fsdp', 'tp')
- value_weight_grad: float32 [2, 8192, 1024], P('pp', 'fsdp', 'tp')
- out_weight_grad: float32 [2, 4096, 8192], P('pp', 'tp', 'fsdp')
Inputs may be any that keep to these rules, and one draw needn't show every extreme that they name: `groups`: every group value names exactly 2 completions.
All inputs are finite; a program needn't handle non-finite values. No bound on the sum of `noise_mask` on one device may be relied on, other than what follows from the above.
Results may differ from a plain program's by a relative error of at most 0.013.
Values may be sent and summed in bfloat16 or wider, within the bound.
A program may use at most 128 MiB of HBM per device.

v0:
```python
import jax
import jax.numpy as jnp
from jax import lax
from jax.sharding import PartitionSpec as P

MODEL_WIDTH = 8192
HEAD_WIDTH = 128
SLOT = 32
epsilon = 1e-06
masked_score = -1e30


def segments(lengths):
    ends = jnp.stack([jnp.sum(lengths[..., : c + 1], -1) for c in range(lengths.shape[-1])], -1)
    position = jnp.arange(SLOT, dtype=jnp.int32)
    return jnp.sum((ends[..., None, :] <= position[:, None]).astype(jnp.int32), -1)


def token_weights(lengths, rewards, groups):
    group_total = 2 * lengths.shape[1]
    reward_flat = rewards.reshape(-1).astype(jnp.float32)
    member = (
        groups.reshape(-1)[:, None] == jnp.arange(group_total, dtype=jnp.int32)[None, :]
    ).astype(jnp.float32)
    member_count = jnp.sum(member, 0)
    group_mean = jnp.sum(member * reward_flat[:, None], 0) / member_count
    centered = reward_flat - jnp.sum(member * group_mean[None, :], 1)
    variance = jnp.sum(member * (centered * centered)[:, None], 0) / member_count
    spread_own = jnp.sum(member * jnp.sqrt(variance)[None, :], 1)
    advantage = (centered / jnp.maximum(spread_own, 1.0)).reshape(lengths.shape)
    segment = segments(lengths)
    choose = (segment[..., None] == jnp.arange(lengths.shape[2], dtype=jnp.int32)).astype(
        jnp.float32
    )
    token_adv = jnp.sum(choose * advantage[:, :, None, :], -1)
    token_len = jnp.sum(choose * lengths[:, :, None, :].astype(jnp.float32), -1)
    return (token_adv * SLOT / token_len).reshape(lengths.shape[0], -1)


def heads_of(rows):
    return rows.reshape(rows.shape[0], -1, HEAD_WIDTH).astype(jnp.float32)


def attend(query_rows, key_rows, value_rows, same_doc):
    keys, values = (heads_of(key_rows), heads_of(value_rows))
    count = keys.shape[1]
    queries = heads_of(query_rows).reshape(SLOT, count, -1, HEAD_WIDTH)
    scores = jnp.einsum("ikgd,jkd->kgij", queries, keys) * HEAD_WIDTH ** (-0.5)
    probs = jax.nn.softmax(jnp.where(same_doc, scores, masked_score), axis=-1)
    mixture = jnp.einsum("kgij,jkd->ikgd", probs.astype(jnp.bfloat16).astype(jnp.float32), values)
    return (mixture.reshape(SLOT, -1).astype(jnp.bfloat16), probs)


def attend_back(query_rows, key_rows, value_rows, probs, head_out_grad):
    keys, values = (heads_of(key_rows), heads_of(value_rows))
    count = keys.shape[1]
    queries = heads_of(query_rows).reshape(SLOT, count, -1, HEAD_WIDTH)
    grads = heads_of(head_out_grad).reshape(queries.shape)
    rounded = probs.astype(jnp.bfloat16).astype(jnp.float32)
    prob_grad = jnp.einsum("ikgd,jkd->kgij", grads, values)
    value_grad = jnp.einsum("kgij,ikgd->jkd", rounded, grads)
    score_grad = probs * (prob_grad - jnp.sum(prob_grad * probs, -1, keepdims=True))
    score_grad = score_grad.astype(jnp.bfloat16).astype(jnp.float32)
    scale = HEAD_WIDTH ** (-0.5)
    query_grad = jnp.einsum("kgij,jkd->ikgd", score_grad, keys) * scale
    key_grad = jnp.einsum("kgij,ikgd->jkd", score_grad, queries) * scale
    return jnp.concatenate(
        [v.reshape(SLOT, -1).astype(jnp.bfloat16) for v in (query_grad, key_grad, value_grad)], 1
    )


def dot(a, b, contract):
    return lax.dot_general(a, b, (contract, ((), ())), preferred_element_type=jnp.float32)


def scatter(value, axis):
    return lax.psum_scatter(value, axis, scatter_dimension=0, tiled=True)


def gather(value, axis):
    return lax.all_gather(value, axis, axis=0, tiled=True)


def local(
    inputs,
    head_grad,
    noise_mask,
    lengths,
    rewards,
    groups,
    query_weight,
    key_weight,
    value_weight,
    out_weight,
):
    core = lax.axis_index("pp")
    row_count = inputs.shape[1]
    query_cols, key_cols = (query_weight.shape[2], key_weight.shape[2])
    cols = query_cols + 2 * key_cols
    own_qkv = jnp.concatenate([query_weight[0], key_weight[0], value_weight[0]], 1)
    own_out = out_weight[0]
    swap = [(0, 1), (1, 0)]
    far_qkv, far_out = (lax.ppermute(own_qkv, "pp", swap), lax.ppermute(own_out, "pp", swap))
    qkv = [jnp.where(core == 0, own_qkv, far_qkv), jnp.where(core == 0, far_qkv, own_qkv)]
    out = [jnp.where(core == 0, own_out, far_out), jnp.where(core == 0, far_out, own_out)]
    segment = segments(lengths)[core, lax.axis_index("fsdp")]
    same_doc = segment[:, None] == segment[None, :]
    weight = lax.dynamic_slice_in_dim(
        token_weights(lengths, rewards, groups)[core],
        lax.axis_index("tp") * row_count,
        row_count,
        0,
    ) * noise_mask[core].astype(jnp.float32)
    top_grad = (-weight[:, None] * head_grad[core].astype(jnp.float32)).astype(jnp.bfloat16)

    def project(stream_all, layer):
        wide = stream_all.astype(jnp.float32)
        squares = jnp.sum(wide * wide, -1, keepdims=True)
        partial = jnp.concatenate(
            [
                dot(stream_all, qkv[layer], ((1,), (0,))),
                jnp.broadcast_to(squares, (squares.shape[0], 128)),
            ],
            1,
        )
        summed = scatter(partial, "fsdp")
        inv_rms = lax.rsqrt(summed[:, cols : cols + 1] / MODEL_WIDTH + epsilon)
        rows = (summed[:, :cols] * inv_rms).astype(jnp.bfloat16)
        return (
            inv_rms,
            rows[:, :query_cols],
            rows[:, query_cols : query_cols + key_cols],
            rows[:, query_cols + key_cols :],
        )

    def head_grads(grad_all, layer):
        return scatter(dot(grad_all, out[layer], ((1,), (1,))), "fsdp").astype(jnp.bfloat16)

    stream0 = inputs[core]
    stream0_all = gather(stream0, "tp")
    grad1_all = gather(top_grad, "tp")
    inv0, q0, k0, v0 = project(stream0_all, 0)
    head_grad1 = head_grads(grad1_all, 1)
    head0, probs0 = attend(q0, k0, v0, same_doc)
    heads0_all = gather(head0, "fsdp")
    stream1 = (
        stream0.astype(jnp.float32) + scatter(dot(heads0_all, out[0], ((1,), (0,))), "tp")
    ).astype(jnp.bfloat16)
    stream1_all = gather(stream1, "tp")
    inv1, q1, k1, v1 = project(stream1_all, 1)
    head1, probs1 = attend(q1, k1, v1, same_doc)
    heads1_all = gather(head1, "fsdp")
    grads1 = attend_back(q1, k1, v1, probs1, head_grad1).astype(jnp.float32)
    rows1 = jnp.concatenate([q1, k1, v1], 1).astype(jnp.float32)
    share = inv1 * jnp.sum(grads1 * rows1, -1, keepdims=True) * inv1 / MODEL_WIDTH
    scaled1 = (grads1 * inv1).astype(jnp.bfloat16)
    scaled1_all = gather(scaled1, "fsdp")
    share_all = gather(jnp.broadcast_to(share, (SLOT, 128)), "fsdp")[:, :1]
    part = dot(scaled1_all, qkv[1], ((1,), (1,))) - stream1_all.astype(jnp.float32) * share_all
    grad0 = (top_grad.astype(jnp.float32) + scatter(part, "tp")).astype(jnp.bfloat16)
    grad0_all = gather(grad0, "tp")
    head_grad0 = head_grads(grad0_all, 0)
    grads0 = attend_back(q0, k0, v0, probs0, head_grad0).astype(jnp.float32)
    scaled0_all = gather((grads0 * inv0).astype(jnp.bfloat16), "fsdp")

    def both(first, second):
        own = jnp.where(core == 0, first, second)
        other = lax.ppermute(jnp.where(core == 0, second, first), "pp", swap)
        return jnp.concatenate([own, other], 0)

    streams = both(stream0_all, stream1_all)
    heads = both(heads0_all, heads1_all)
    out_grads = both(grad0_all, grad1_all)
    scaled = both(scaled0_all, scaled1_all)
    qkv_grad = dot(streams, scaled, ((0,), (0,)))
    return (
        qkv_grad[None, :, :query_cols],
        qkv_grad[None, :, query_cols : query_cols + key_cols],
        qkv_grad[None, :, query_cols + key_cols :],
        dot(heads, out_grads, ((0,), (0,)))[None],
    )


def solution(mesh):
    return jax.shard_map(
        local,
        mesh=mesh,
        in_specs=(
            P(None, "tp", "fsdp"),
            P(None, "tp", "fsdp"),
            P(None, "tp"),
            P(),
            P(),
            P(),
            P("pp", "fsdp", "tp"),
            P("pp", "fsdp", "tp"),
            P("pp", "fsdp", "tp"),
            P("pp", "tp", "fsdp"),
        ),
        out_specs=(
            P("pp", "fsdp", "tp"),
            P("pp", "fsdp", "tp"),
            P("pp", "fsdp", "tp"),
            P("pp", "tp", "fsdp"),
        ),
        check_vma=False,
    )
```

profile of v0, /device:TPU:1, one launch (start us, length us, event | category | flops | bytes accessed | tf_op | source)
XLA Modules:
  0.0 620.1 jit_solution(6315300125879777344)
XLA Ops:
  7.2 1.6 pad_maximum_fusion.2
  8.8 1.5 collective-permute-start
  10.4 12.3 %all-gather = bf16[1,512,512]{2,1,0:T(8,128)(2,1)S(1)} all-gather(bf16[1,128,512]{2,1,0:T(8,128)(2,1)S(1)} %constant_dynamic-slice_fusion.2), channel_id=3, replica_groups=mesh['pp'=2,'fsdp'=16,'tp'=4] {'tp'}, dimensions={1}, use_global_device_ids=true | all-gather | bytes 655360 | tf_op jit(solution)/shard_map/all_gather | solution.py:81
  22.9 2.5 fusion.13
  25.5 2.0 pad_maximum_fusion
  27.5 0.6 copy-done.21
  28.4 76.2 %reduce-scatter.7.cloned.1.call-done = f32[32,1664]{1,0:T(8,128)} async-done(((f32[512,1664]{1,0:T(8,128)}), f32[32,1664]{1,0:T(8,128)}) %reduce-scatter.7.cloned.1.call-update) | async-done | bytes 213008 | tf_op jit(solution)/shard_map/reduce_scatter | solution.py:77
  104.6 0.8 fusion.78
  105.4 1.0 fusion.59
  106.8 0.6 copy-done.11
  107.7 0.7 convert_element_type.203
  108.5 2.5 collective-permute-start.1
  111.7 1.5 collective-permute-done.1
  113.2 37.5 %all-gather.7.cloned.1.call-done = bf16[512,1024]{1,0:T(8,128)(2,1)} async-done(((bf16[32,1024]{1,0:T(8,128)(2,1)}), bf16[512,1024]{1,0:T(8,128)(2,1)}) %all-gather.7.cloned.1.call-update) | async-done | bytes 1048592 | tf_op jit(solution)/shard_map/all_gather | solution.py:81
  150.7 2.9 fusion.53
  154.5 11.4 %all_gather.30 = bf16[512,512]{1,0:T(8,128)(2,1)S(1)} all-gather(bf16[128,512]{1,0:T(8,128)(2,1)S(1)} %fusion.54), channel_id=1, replica_groups=mesh['pp'=2,'fsdp'=16,'tp'=4] {'tp'}, dimensions={0}, use_global_device_ids=true | all-gather | bytes 655360 | tf_op jit(solution)/shard_map/all_gather | solution.py:81
  165.9 2.1 fusion.47
  168.1 9.5 %reduce-scatter.9.cloned.1.call-done = f32[128,512]{1,0:T(8,128)} async-done(((f32[512,512]{1,0:T(8,128)}), f32[128,512]{1,0:T(8,128)}) %reduce-scatter.9.cloned.1.call-update) | async-done | bytes 262160 | tf_op jit(solution)/shard_map/reduce_scatter | solution.py:77
  177.5 1.0 fusion.55
  178.5 10.3 %all_gather.29 = bf16[512,512]{1,0:T(8,128)(2,1)S(1)} all-gather(bf16[128,512]{1,0:T(8,128)(2,1)S(1)} %fusion.55), channel_id=1, replica_groups=mesh['pp'=2,'fsdp'=16,'tp'=4] {'tp'}, dimensions={0}, use_global_device_ids=true | all-gather | bytes 655360 | tf_op jit(solution)/shard_map/all_gather | solution.py:81
  189.0 2.3 fusion.50
  191.4 2.0 pad_maximum_fusion.1
  193.4 61.5 %reduce-scatter.13.cloned.1.call-done = f32[32,1024]{1,0:T(8,128)} async-done(((f32[512,1024]{1,0:T(8,128)}), f32[32,1024]{1,0:T(8,128)}) %reduce-scatter.13.cloned.1.call-update) | async-done | bytes 131088 | tf_op jit(solution)/shard_map/reduce_scatter | solution.py:77
  255.0 0.9 convert_element_type.216
  255.9 0.7 reshape.148
  256.6 77.0 %reduce-scatter.11.cloned.1.call-done = f32[32,1664]{1,0:T(8,128)} async-done(((f32[512,1664]{1,0:T(8,128)}), f32[32,1664]{1,0:T(8,128)}) %reduce-scatter.11.cloned.1.call-update) | async-done | bytes 213008 | tf_op jit(solution)/shard_map/reduce_scatter | solution.py:77
  333.5 0.9 fusion.87
  334.4 1.0 fusion.58
  335.5 0.6 slice.70
  336.1 0.9 reshape.146
  337.0 1.6 fusion.128
  338.6 1.2 multiply_reduce_fusion.2
  339.8 0.9 multiply_convert_fusion.2
  340.9 0.4 fusion.39
  341.3 1.9 fusion.38
  343.2 0.7 convert_element_type.220
  343.9 0.7 copy.219
  344.6 1.7 fusion.57
  346.4 1.2 dynamic-slice.1
  348.8 30.9 %all-reduce = f32[512]{0:T(512)S(1)} all-reduce(f32[512]{0:T(512)S(1)} %dynamic-update-slice), channel_id=4, replica_groups=mesh['pp'=2,'fsdp'=16,'tp'=4] {'fsdp'}, use_global_device_ids=true, to_apply=%add | all-reduce | flops 512 | bytes 4096
  379.7 10.6 %all-gather.9.cloned.1.call-done = bf16[512,1536]{1,0:T(8,128)(2,1)} async-done(((bf16[32,1536]{1,0:T(8,128)(2,1)}), bf16[512,1536]{1,0:T(8,128)(2,1)}) %all-gather.9.cloned.1.call-update) | async-done | bytes 1572880 | tf_op jit(solution)/shard_map/all_gather | solution.py:81
  390.4 3.7 convolution_subtract_fusion
  394.1 22.9 %reduce-scatter.15.cloned.1.call-done = f32[128,512]{1,0:T(8,128)} async-done(((f32[512,512]{1,0:T(8,128)}), f32[128,512]{1,0:T(8,128)}) %reduce-scatter.15.cloned.1.call-update) | async-done | bytes 262160 | tf_op jit(solution)/shard_map/reduce_scatter | solution.py:77
  417.0 1.1 add_convert_fusion
  418.1 11.1 %all_gather.33 = bf16[512,512]{1,0:T(8,128)(2,1)S(1)} all-gather(bf16[128,512]{1,0:T(8,128)(2,1)S(1)} %add_convert_fusion), channel_id=1, replica_groups=mesh['pp'=2,'fsdp'=16,'tp'=4] {'tp'}, dimensions={0}, use_global_device_ids=true | all-gather | bytes 655360 | tf_op jit(solution)/shard_map/all_gather | solution.py:81
  429.2 3.3 fusion.52
  432.6 74.5 %reduce-scatter.17.cloned.1.call-done = f32[32,1024]{1,0:T(8,128)} async-done(((f32[512,1024]{1,0:T(8,128)}), f32[32,1024]{1,0:T(8,128)}) %reduce-scatter.17.cloned.1.call-update) | async-done | bytes 131088 | tf_op jit(solution)/shard_map/reduce_scatter | solution.py:77
  507.1 0.9 convert_element_type.232
  508.9 0.4 fusion.36
  509.4 0.7 multiply_convert_fusion
  510.5 0.7 convert_element_type.247
  511.2 43.0 %all-gather.11.cloned.1.call-done = bf16[512,1536]{1,0:T(8,128)(2,1)} async-done(((bf16[32,1536]{1,0:T(8,128)(2,1)}), bf16[512,1536]{1,0:T(8,128)(2,1)}) %all-gather.11.cloned.1.call-update) | async-done | bytes 1572880 | tf_op jit(solution)/shard_map/all_gather | solution.py:81
  554.2 3.8 broadcast_select_fusion.1
  557.9 1.6 collective-permute-start.3
  559.6 38.7 %all-gather.13.cloned.1.call-done = bf16[512,1024]{1,0:T(8,128)(2,1)} async-done(((bf16[32,1024]{1,0:T(8,128)(2,1)}), bf16[512,1024]{1,0:T(8,128)(2,1)}) %all-gather.13.cloned.1.call-update) | async-done | bytes 1048592 | tf_op jit(solution)/shard_map/all_gather | solution.py:81
  598.3 1.4 broadcast_select_fusion.4
  599.6 2.2 collective-permute-start.4
  602.1 0.8 collective-permute-start.2
  602.8 1.3 collective-permute-done.4
  604.1 0.7 collective-permute-done.5
  604.9 2.6 fusion.10
  607.5 3.3 fusion.2
  610.7 1.5 slice_bitcast_fusion
  612.2 1.0 slice_bitcast_fusion.1
  (151 shorter events, 5.8 us)
Async XLA Ops:
  7.2 3.2 copy-start.8
  7.2 97.4 %reduce-scatter.7.cloned.1.call-start = ((), (), s32[]{:S(2)}) async-start(), calls=%async_computation.6 | async-start | bytes 3620864 | tf_op jit(solution)/shard_map/reduce_scatter | solution.py:77
  7.2 15.6 %copy-start.3 = (bf16[1,512,1024]{2,1,0:T(8,128)(2,1)S(1)}, bf16[1,512,1024]{2,1,0:T(8,128)(2,1)}, u32[]{:S(2)}) copy-start(bf16[1,512,1024]{2,1,0:T(8,128)(2,1)} %param.16) | copy-start | bytes 3145732
  7.2 15.6 %copy-start.6 = (bf16[1,512,256]{2,1,0:T(8,128)(2,1)S(1)}, bf16[1,512,256]{2,1,0:T(8,128)(2,1)}, u32[]{:S(2)}) copy-start(bf16[1,512,256]{2,1,0:T(8,128)(2,1)} %param.18) | copy-start | bytes 786436
  8.8 14.0 %collective-permute-start = (bf16[512,1536]{1,0:T(8,128)(2,1)S(1)}, bf16[512,1536]{1,0:T(8,128)(2,1)}, u32[]{:S(2)}, u32[]{:S(2)}) collective-permute-start(bf16[512,1536]{1,0:T(8,128)(2,1)S(1)} %pad_maximum_fusion.2), channel_id=1, source_target_pairs={{0,64},{64,0},{1,65},{65,1},{2,66},{66,2},{3,67},{67,3},{4,68},{68... | collective-permute-start | bytes 4718600 | tf_op jit(solution)/shard_map/ppermute | solution.py:103
  27.4 0.7 copy-start.21
  27.4 0.8 slice-start
  27.4 81.0 %copy-start = (bf16[1,1024,512]{2,1,0:T(8,128)(2,1)S(1)}, bf16[1,1024,512]{2,1,0:T(8,128)(2,1)}, u32[]{:S(2)}) copy-start(bf16[1,1024,512]{2,1,0:T(8,128)(2,1)} %param.19) | copy-start | bytes 3145732
  27.4 83.5 %copy-start.29 = (s32[2,16,2]{1,2,0:T(2,128)S(1)}, s32[2,16,2]{1,2,0:T(2,128)}, u32[]{:S(2)}) copy-start(s32[2,16,2]{1,2,0:T(2,128)} %param.15) | copy-start | bytes 772
  27.5 83.7 %copy-start.30 = (s32[2,16,2]{1,2,0:T(2,128)S(1)}, s32[2,16,2]{1,2,0:T(2,128)}, u32[]{:S(2)}) copy-start(s32[2,16,2]{1,2,0:T(2,128)} %param.14) | copy-start | bytes 772
  27.5 123.2 %all-gather.7.cloned.1.call-start = ((), (), s32[]{:S(2)}) async-start(), calls=%async_computation.7 | async-start | bytes 1114112 | tf_op jit(solution)/shard_map/all_gather | solution.py:81
  28.4 78.5 %copy-start.28 = (pred[32,32]{0,1:T(8,128)(4,1)}, pred[32,32]{0,1:T(8,128)(4,1)S(1)}, u32[]{:S(2)}) copy-start(pred[32,32]{0,1:T(8,128)(4,1)S(1)} %broadcast_compare_fusion) | copy-start | bytes 3076
  105.4 48.2 %copy-start.18 = (f32[32]{0:T(128)}, f32[32]{0:T(128)S(1)}, u32[]{:S(2)}) copy-start(f32[32]{0:T(128)S(1)} %fusion.78) | copy-start | bytes 388
  106.5 5.1 copy-start.14
  106.8 0.7 copy-start.11
  106.8 4.9 copy-start.24
  108.4 69.1 %reduce-scatter.9.cloned.1.call-start = ((), (), s32[]{:S(2)}) async-start(), calls=%async_computation.8 | async-start | bytes 1310720 | tf_op jit(solution)/shard_map/reduce_scatter | solution.py:77
  108.5 4.8 collective-permute-start.1
  111.7 42.6 %copy-start.31 = (s32[2,128]{1,0:T(2,128)S(1)}, s32[2,128]{1,0:T(2,128)}, u32[]{:S(2)}) copy-start(s32[2,128]{1,0:T(2,128)} %param.12) | copy-start | bytes 3076
  111.7 42.7 %copy-start.10 = (bf16[2,128,512]{2,1,0:T(8,128)(2,1)S(1)}, bf16[2,128,512]{2,1,0:T(8,128)(2,1)}, u32[]{:S(2)}) copy-start(bf16[2,128,512]{2,1,0:T(8,128)(2,1)} %param.11) | copy-start | bytes 786436
  113.2 52.7 %copy-start.1 = (bf16[1024,512]{1,0:T(8,128)(2,1)}, bf16[1024,512]{1,0:T(8,128)(2,1)S(1)}, u32[]{:S(2)}) copy-start(bf16[1024,512]{1,0:T(8,128)(2,1)S(1)} %collective-permute-done.1) | copy-start | bytes 3145732
  153.7 101.3 %reduce-scatter.13.cloned.1.call-start = ((), (), s32[]{:S(2)}) async-start(), calls=%async_computation.10 | async-start | bytes 2228224 | tf_op jit(solution)/shard_map/reduce_scatter | solution.py:77
  154.4 13.5 %copy-start.22 = (f32[128]{0:T(128)}, f32[128]{0:T(128)S(1)}, u32[]{:S(2)}) copy-start(f32[128]{0:T(128)S(1)} %fusion.100) | copy-start | bytes 1540
  168.0 9.6 %copy-start.9 = (bf16[2,128,512]{2,1,0:T(8,128)(2,1)S(1)}, bf16[2,128,512]{2,1,0:T(8,128)(2,1)}, u32[]{:S(2)}) copy-start(bf16[2,128,512]{2,1,0:T(8,128)(2,1)} %param.10) | copy-start | bytes 786436
  168.0 21.0 %copy-start.7 = (bf16[1,512,256]{2,1,0:T(8,128)(2,1)S(1)}, bf16[1,512,256]{2,1,0:T(8,128)(2,1)}, u32[]{:S(2)}) copy-start(bf16[1,512,256]{2,1,0:T(8,128)(2,1)} %param.17) | copy-start | bytes 786436
  168.0 165.5 %reduce-scatter.11.cloned.1.call-start = ((), (), s32[]{:S(2)}) async-start(), calls=%async_computation.9 | async-start | bytes 3620864 | tf_op jit(solution)/shard_map/reduce_scatter | solution.py:77
  193.4 197.0 %all-gather.9.cloned.1.call-start = ((), (), s32[]{:S(2)}) async-start(), calls=%async_computation.11 | async-start | bytes 1671168 | tf_op jit(solution)/shard_map/all_gather | solution.py:81
  333.5 11.1 %copy-start.5 = (f32[32,1664]{1,0:T(8,128)S(1)}, f32[32,1664]{1,0:T(8,128)}, u32[]{:S(2)}) copy-start(f32[32,1664]{1,0:T(8,128)} %reduce-scatter.11.cloned.1.call-done) | copy-start | bytes 638980
  334.4 2.5 copy-start.20
  337.0 57.0 %copy-start.16 = (bf16[32,2,128]{2,1,0:T(2,128)(2,1)}, bf16[32,2,128]{2,1,0:T(2,128)(2,1)S(1)}, u32[]{:S(2)}) copy-start(bf16[32,2,128]{2,1,0:T(2,128)(2,1)S(1)} %reshape.147) | copy-start | bytes 49156
  338.6 4.6 copy-start.26
  346.4 70.7 %reduce-scatter.15.cloned.1.call-start = ((), (), s32[]{:S(2)}) async-start(), calls=%async_computation.12 | async-start | bytes 1310720 | tf_op jit(solution)/shard_map/reduce_scatter | solution.py:77
  379.7 37.3 %copy-start.23 = (f32[128]{0:T(128)S(1)}, f32[128]{0:T(128)}, u32[]{:S(2)}) copy-start(f32[128]{0:T(128)} %copy-done.22) | copy-start | bytes 1540
  394.1 113.0 %reduce-scatter.17.cloned.1.call-start = ((), (), s32[]{:S(2)}) async-start(), calls=%async_computation.13 | async-start | bytes 2228224 | tf_op jit(solution)/shard_map/reduce_scatter | solution.py:77
  432.5 75.6 %copy-start.12 = (f32[2,4,32,32]{2,3,1,0:T(8,128)S(1)}, f32[2,4,32,32]{2,3,1,0:T(8,128)}, u32[]{:S(2)}) copy-start(f32[2,4,32,32]{2,3,1,0:T(8,128)} %copy-done.11) | copy-start | bytes 98308
  432.5 75.6 %copy-start.15 = (bf16[32,2,128]{2,1,0:T(2,128)(2,1)S(1)}, bf16[32,2,128]{2,1,0:T(2,128)(2,1)}, u32[]{:S(2)}) copy-start(bf16[32,2,128]{2,1,0:T(2,128)(2,1)} %copy-done.14) | copy-start | bytes 49156
  432.5 75.6 %copy-start.25 = (f32[2,4,32]{2,1,0:T(4,128)S(1)}, f32[2,4,32]{2,1,0:T(4,128)}, u32[]{:S(2)}) copy-start(f32[2,4,32]{2,1,0:T(4,128)} %copy-done.24) | copy-start | bytes 3076
  432.5 76.9 %copy-start.19 = (f32[32]{0:T(128)S(1)}, f32[32]{0:T(128)}, u32[]{:S(2)}) copy-start(f32[32]{0:T(128)} %copy-done.18) | copy-start | bytes 388
  432.5 77.8 %copy-start.13 = (f32[2,4,32,32]{2,3,1,0:T(8,128)S(1)}, f32[2,4,32,32]{2,3,1,0:T(8,128)}, u32[]{:S(2)}) copy-start(f32[2,4,32,32]{2,3,1,0:T(8,128)} %get-tuple-element.29) | copy-start | bytes 98308
  432.5 77.7 %copy-start.17 = (bf16[32,2,128]{2,1,0:T(2,128)(2,1)S(1)}, bf16[32,2,128]{2,1,0:T(2,128)(2,1)}, u32[]{:S(2)}) copy-start(bf16[32,2,128]{2,1,0:T(2,128)(2,1)} %copy-done.16) | copy-start | bytes 49156
  432.5 77.7 %copy-start.27 = (f32[2,4,32]{2,1,0:T(4,128)S(1)}, f32[2,4,32]{2,1,0:T(4,128)}, u32[]{:S(2)}) copy-start(f32[2,4,32]{2,1,0:T(4,128)} %copy-done.26) | copy-start | bytes 3076
  432.5 121.6 %all-gather.11.cloned.1.call-start = ((), (), s32[]{:S(2)}) async-start(), calls=%async_computation.14 | async-start | bytes 1671168 | tf_op jit(solution)/shard_map/all_gather | solution.py:81
  510.2 88.1 %all-gather.13.cloned.1.call-start = ((), (), s32[]{:S(2)}) async-start(), calls=%async_computation.15 | async-start | bytes 1114112 | tf_op jit(solution)/shard_map/all_gather | solution.py:81
  511.2 87.1 %copy-start.4 = (bf16[512,1024]{1,0:T(8,128)(2,1)S(1)}, bf16[512,1024]{1,0:T(8,128)(2,1)}, u32[]{:S(2)}) copy-start(bf16[512,1024]{1,0:T(8,128)(2,1)} %all-gather.7.cloned.1.call-done) | copy-start | bytes 3145732
  557.9 49.5 %collective-permute-start.3 = (bf16[512,1536]{1,0:T(8,128)(2,1)}, bf16[512,1536]{1,0:T(8,128)(2,1)}, u32[]{:S(2)}, u32[]{:S(2)}) collective-permute-start(bf16[512,1536]{1,0:T(8,128)(2,1)} %get-tuple-element.11), channel_id=1, source_target_pairs={{0,64},{64,0},{1,65},{65,1},{2,66},{66,2},{3,67},{67,3},{4,68},{68... | collective-permute-start | bytes 4718600 | tf_op jit(solution)/shard_map/ppermute | solution.py:168
  599.6 4.5 collective-permute-start.4
  601.9 3.0 collective-permute-start.5
  602.1 5.4 collective-permute-start.2
  604.9 2.6 copy-start.2
Sparse Core Ops, SparseCore 0:
  27.6 76.9 reduce-scatter.6
  108.5 42.1 all-gather.6
  153.8 23.7 reduce-scatter.8
  181.6 73.3 reduce-scatter.12
  258.2 75.3 reduce-scatter.10
  346.5 43.8 all-gather.8
  394.2 22.7 reduce-scatter.14
  432.7 74.4 reduce-scatter.16
  510.3 43.8 all-gather.10
  556.7 41.4 all-gather.12
where the time goes:
time: 621 us; the launch traced here: 620 us
  waiting for transfers between devices  455 us (73%)
  blocking collectives  76 us (12%)
  matrix products  29.6 us (5%)
  other arithmetic  23.1 us (4%)
  between operations  15.4 us (2%)
  local copies, waits for them, and re-layouts  11.7 us (2%)
  starting transfers between devices  9.02 us (1%)
    reduce_scatter x6, waiting for transfers between devices, scatter(): return lax.psum_scatter(value, axis, scatter_dimension=0, tiled=True)  322 us
    all_gather x4, waiting for transfers between devices, gather(): return lax.all_gather(value, axis, axis=0, tiled=True)  130 us
    all_gather x4, blocking collectives, gather(): return lax.all_gather(value, axis, axis=0, tiled=True)  45 us
    unnamed x1, blocking collectives  30.9 us
    dot_general x8, matrix products, dot(): lax.dot_general(a, b, (contract, ((), ())), preferred_element_type=jnp.fl...  22.5 us
  transfers between devices with their start and end apart: 16, of which 13 were waited for; matrix products, arithmetic and copies ran while one was open for 3% of the time, Pallas kernels for 0%

commit v1 on v0

--- a/solution.py
+++ b/solution.py
@@ -78,7 +78,9 @@
 
 
 def gather(value, axis):
-    return lax.all_gather(value, axis, axis=0, tiled=True)
+    return jnp.concatenate(
+        lax.all_to_all(jnp.stack([value] * lax.axis_size(axis)), axis, 0, 0), axis=0
+    )
 
 
 def local(

time: 621 us -> 543 us (0.87)
  waiting for transfers between devices: 455 us -> 384 us
  blocking collectives: 76 us -> 48.3 us
  starting transfers between devices: 9.02 us -> 35 us
  matrix products: 29.6 us -> 20.5 us
    all_gather x4 -> x0, waiting for transfers between devices: 130 us -> none  [gather(): return lax.all_gather(value, axis, axis=0, tiled=True)]
    all_to_all x0 -> x5, waiting for transfers between devices: none -> 71.1 us  [gather(): lax.all_to_all(jnp.stack([value] * lax.axis_size(axis)), axis, 0, 0)]
    all_to_all x0 -> x4, blocking collectives: none -> 48.3 us  [gather(): lax.all_to_all(jnp.stack([value] * lax.axis_size(axis)), axis, 0, 0)]
    all_gather x4 -> x0, blocking collectives: 45 us -> none  [gather(): return lax.all_gather(value, axis, axis=0, tiled=True)]
    unnamed x1 -> x0, blocking collectives: 30.9 us -> none
    all_to_all x0 -> x5, starting transfers between devices: none -> 24 us  [gather(): lax.all_to_all(jnp.stack([value] * lax.axis_size(axis)), axis, 0, 0)]
    reduce_scatter x6, waiting for transfers between devices: 322 us -> 312 us  [scatter(): return lax.psum_scatter(value, axis, scatter_dimension=0, tiled=True)]
  transfers between devices with their start and end apart: 16 -> 17, of which waited for: 13 -> 13; matrix products, arithmetic and copies ran while one was open for 3% -> 5% of each run, Pallas kernels for 0% -> 0%
where the time goes in v1:
time: 543 us; the launch traced here: 541 us
  waiting for transfers between devices  384 us (71%)
  blocking collectives  48.3 us (9%)
  starting transfers between devices  35 us (6%)
  other arithmetic  22.9 us (4%)
  matrix products  20.5 us (4%)
  local copies, waits for them, and re-layouts  15.5 us (3%)
  between operations  14.8 us (3%)
    reduce_scatter x6, waiting for transfers between devices, scatter(): return lax.psum_scatter(value, axis, scatter_dimension=0, tiled=True)  312 us
    all_to_all x5, waiting for transfers between devices, gather(): lax.all_to_all(jnp.stack([value] * lax.axis_size(axis)), axis, 0, 0)  71.1 us
    all_to_all x4, blocking collectives, gather(): lax.all_to_all(jnp.stack([value] * lax.axis_size(axis)), axis, 0, 0)  48.3 us
    all_to_all x5, starting transfers between devices, gather(): lax.all_to_all(jnp.stack([value] * lax.axis_size(axis)), axis, 0, 0)  24 us
    dot_general x8, matrix products, dot(): lax.dot_general(a, b, (contract, ((), ())), preferred_element_type=jnp.fl...  17.2 us
  transfers between devices with their start and end apart: 17, of which 13 were waited for; matrix products, arithmetic and copies ran while one was open for 5% of the time, Pallas kernels for 0%

profile of v1, /device:TPU:1, one launch (start us, length us, event | category | flops | bytes accessed | tf_op | source)
XLA Modules:
  0.0 541.5 jit_solution(14457810378640062822)
XLA Ops:
  7.2 1.6 pad_maximum_fusion.2
  8.8 1.5 collective-permute-start
  10.3 0.8 stack.24
  11.2 5.1 all-to-all-start
  16.3 9.3 %all-to-all-done = bf16[4,128,512]{2,1,0:T(8,128)(2,1)S(1)} async-done(((bf16[4,128,512]{2,1,0:T(8,128)(2,1)}), bf16[4,128,512]{2,1,0:T(8,128)(2,1)S(1)}, u32[]{:S(2)}, u32[]{:S(2)}) %all-to-all-start) | async-done | bytes 524320 | tf_op jit(solution)/shard_map/all_to_all | solution.py:82
  25.8 2.4 fusion.13
  28.4 2.0 pad_maximum_fusion
  30.4 1.2 copy-done.8
  31.6 0.7 collective-permute-start.1
  33.0 71.4 %reduce-scatter.7.cloned.1.call-done = f32[32,1664]{1,0:T(8,128)} async-done(((f32[512,1664]{1,0:T(8,128)}), f32[32,1664]{1,0:T(8,128)}) %reduce-scatter.7.cloned.1.call-update) | async-done | bytes 213008 | tf_op jit(solution)/shard_map/reduce_scatter | solution.py:77
  104.4 0.8 fusion.78
  105.8 1.0 fusion.58
  108.1 1.1 stack.27
  109.2 4.7 all-to-all-start.1
  114.9 14.0 %all-to-all-done.1 = bf16[16,32,1024]{2,1,0:T(8,128)(2,1)S(1)} async-done(((bf16[16,32,1024]{2,1,0:T(8,128)(2,1)}), bf16[16,32,1024]{2,1,0:T(8,128)(2,1)S(1)}, u32[]{:S(2)}, u32[]{:S(2)}) %all-to-all-start.1) | async-done | bytes 1048608 | tf_op jit(solution)/shard_map/all_to_all | solution.py:82
  128.9 1.7 fusion.51
  131.3 0.7 max.15
  132.0 0.6 subtract_divide_fusion
  132.6 0.8 copy.123
  133.4 0.8 select_reduce_fusion.1
  134.3 0.8 fusion.100
  135.1 1.0 fusion.59
  136.1 17.6 %all_to_all.45 = bf16[4,128,512]{2,1,0:T(8,128)(2,1)S(1)} all-to-all(bf16[4,128,512]{2,1,0:T(8,128)(2,1)S(1)} %stack.30), channel_id=1, replica_groups=mesh['pp'=2,'fsdp'=16,'tp'=4] {'tp'}, dimensions={0} | all-to-all | bytes 1048576 | tf_op jit(solution)/shard_map/all_to_all | solution.py:82
  153.7 0.8 copy-done
  154.5 2.1 fusion.46
  156.6 1.2 reduce-scatter.9.cloned.1.call-done
  157.8 1.0 add_convert_fusion.1
  158.8 9.3 %all_to_all.46 = bf16[4,128,512]{2,1,0:T(8,128)(2,1)S(1)} all-to-all(bf16[4,128,512]{2,1,0:T(8,128)(2,1)S(1)} %stack.28), channel_id=1, replica_groups=mesh['pp'=2,'fsdp'=16,'tp'=4] {'tp'}, dimensions={0} | all-to-all | bytes 1048576 | tf_op jit(solution)/shard_map/all_to_all | solution.py:82
  168.4 1.0 fusion.49
  169.5 2.0 pad_maximum_fusion.1
  171.5 61.9 %reduce-scatter.13.cloned.1.call-done = f32[32,1024]{1,0:T(8,128)} async-done(((f32[512,1024]{1,0:T(8,128)}), f32[32,1024]{1,0:T(8,128)}) %reduce-scatter.13.cloned.1.call-update) | async-done | bytes 131088 | tf_op jit(solution)/shard_map/reduce_scatter | solution.py:77
  233.4 0.9 convert_element_type.240
  234.4 77.6 %reduce-scatter.11.cloned.1.call-done = f32[32,1664]{1,0:T(8,128)} async-done(((f32[512,1664]{1,0:T(8,128)}), f32[32,1664]{1,0:T(8,128)}) %reduce-scatter.11.cloned.1.call-update) | async-done | bytes 213008 | tf_op jit(solution)/shard_map/reduce_scatter | solution.py:77
  312.0 0.9 fusion.87
  312.9 1.0 fusion.57
  316.1 12.0 %all_to_all.47 = f32[16,32,128]{2,1,0:T(8,128)S(1)} all-to-all(f32[16,32,128]{2,1,0:T(8,128)S(1)} %stack.32), channel_id=1, replica_groups=mesh['pp'=2,'fsdp'=16,'tp'=4] {'fsdp'}, dimensions={0} | all-to-all | bytes 524288 | tf_op jit(solution)/shard_map/all_to_all | solution.py:82
  328.2 1.3 stack.31
  329.5 3.7 all-to-all-start.4
  333.4 19.4 %all-to-all-done.4 = bf16[16,32,1536]{2,1,0:T(8,128)(2,1)S(1)} async-done(((bf16[16,32,1536]{2,1,0:T(8,128)(2,1)}), bf16[16,32,1536]{2,1,0:T(8,128)(2,1)S(1)}, u32[]{:S(2)}, u32[]{:S(2)}) %all-to-all-start.4) | async-done | bytes 1572896 | tf_op jit(solution)/shard_map/all_to_all | solution.py:82
  352.7 3.4 convolution_subtract_fusion
  356.2 24.1 %reduce-scatter.15.cloned.1.call-done = f32[128,512]{1,0:T(8,128)} async-done(((f32[512,512]{1,0:T(8,128)}), f32[128,512]{1,0:T(8,128)}) %reduce-scatter.15.cloned.1.call-update) | async-done | bytes 262160 | tf_op jit(solution)/shard_map/reduce_scatter | solution.py:77
  380.3 1.1 add_convert_fusion
  381.5 9.3 %all_to_all.48 = bf16[4,128,512]{2,1,0:T(8,128)(2,1)S(1)} all-to-all(bf16[4,128,512]{2,1,0:T(8,128)(2,1)S(1)} %stack.33), channel_id=1, replica_groups=mesh['pp'=2,'fsdp'=16,'tp'=4] {'tp'}, dimensions={0} | all-to-all | bytes 1048576 | tf_op jit(solution)/shard_map/all_to_all | solution.py:82
  390.8 0.8 copy-done.2
  391.6 2.1 fusion.50
  393.7 75.4 %reduce-scatter.17.cloned.1.call-done = f32[32,1024]{1,0:T(8,128)} async-done(((f32[512,1024]{1,0:T(8,128)}), f32[32,1024]{1,0:T(8,128)}) %reduce-scatter.17.cloned.1.call-update) | async-done | bytes 131088 | tf_op jit(solution)/shard_map/reduce_scatter | solution.py:77
  469.1 0.9 convert_element_type.257
  471.6 1.3 stack.34
  472.9 4.4 all-to-all-start.7
  477.6 19.5 %all-to-all-done.7 = bf16[16,32,1536]{2,1,0:T(8,128)(2,1)S(1)} async-done(((bf16[16,32,1536]{2,1,0:T(8,128)(2,1)}), bf16[16,32,1536]{2,1,0:T(8,128)(2,1)S(1)}, u32[]{:S(2)}, u32[]{:S(2)}) %all-to-all-start.7) | async-done | bytes 1572896 | tf_op jit(solution)/shard_map/all_to_all | solution.py:82
  497.1 1.1 stack.35
  498.2 6.0 %all-to-all-start.8 = ((bf16[16,32,1024]{2,1,0:T(8,128)(2,1)}), bf16[16,32,1024]{2,1,0:T(8,128)(2,1)}, u32[]{:S(2)}, u32[]{:S(2)}) async-start(bf16[16,32,1024]{2,1,0:T(8,128)(2,1)} %stack.35), calls=%async_computation.14 | async-start | bytes 2097152 | tf_op jit(solution)/shard_map/all_to_all | solution.py:82
  504.2 2.1 bitcast_select_fusion.1
  506.3 3.3 collective-permute-start.3
  509.6 8.9 %all-to-all-done.8 = bf16[16,32,1024]{2,1,0:T(8,128)(2,1)} async-done(((bf16[16,32,1024]{2,1,0:T(8,128)(2,1)}), bf16[16,32,1024]{2,1,0:T(8,128)(2,1)}, u32[]{:S(2)}, u32[]{:S(2)}) %all-to-all-start.8) | async-done | bytes 1048608 | tf_op jit(solution)/shard_map/all_to_all | solution.py:82
  518.5 1.7 bitcast_select_fusion.3
  520.2 4.4 collective-permute-start.4
  525.0 0.9 collective-permute-start.2
  525.9 1.0 collective-permute-done.4
  526.9 0.7 collective-permute-done.5
  527.6 2.6 fusion.10
  530.2 1.9 fusion.2
  532.1 1.5 slice_bitcast_fusion
  533.6 1.0 slice_bitcast_fusion.1
  (163 shorter events, 9.6 us)
Async XLA Ops:
  7.2 3.1 copy-start.18
  7.2 18.6 %copy-start.13 = (bf16[1,512,1024]{2,1,0:T(8,128)(2,1)S(1)}, bf16[1,512,1024]{2,1,0:T(8,128)(2,1)}, u32[]{:S(2)}) copy-start(bf16[1,512,1024]{2,1,0:T(8,128)(2,1)} %param.16) | copy-start | bytes 3145732
  7.2 18.6 %copy-start.16 = (bf16[1,512,256]{2,1,0:T(8,128)(2,1)S(1)}, bf16[1,512,256]{2,1,0:T(8,128)(2,1)}, u32[]{:S(2)}) copy-start(bf16[1,512,256]{2,1,0:T(8,128)(2,1)} %param.18) | copy-start | bytes 786436
  8.8 16.9 %collective-permute-start = (bf16[512,1536]{1,0:T(8,128)(2,1)S(1)}, bf16[512,1536]{1,0:T(8,128)(2,1)}, u32[]{:S(2)}, u32[]{:S(2)}) collective-permute-start(bf16[512,1536]{1,0:T(8,128)(2,1)S(1)} %pad_maximum_fusion.2), channel_id=1, source_target_pairs={{0,64},{64,0},{1,65},{65,1},{2,66},{66,2},{3,67},{67,3},{4,68},{68... | collective-permute-start | bytes 4718600 | tf_op jit(solution)/shard_map/ppermute | solution.py:105
  11.2 14.4 %all-to-all-start = ((bf16[4,128,512]{2,1,0:T(8,128)(2,1)}), bf16[4,128,512]{2,1,0:T(8,128)(2,1)S(1)}, u32[]{:S(2)}, u32[]{:S(2)}) async-start(bf16[4,128,512]{2,1,0:T(8,128)(2,1)} %stack.24), calls=%async_computation | async-start | bytes 1048576 | tf_op jit(solution)/shard_map/all_to_all | solution.py:82
  16.3 88.2 %reduce-scatter.7.cloned.1.call-start = ((), (), s32[]{:S(2)}) async-start(), calls=%async_computation.15 | async-start | bytes 3620864 | tf_op jit(solution)/shard_map/reduce_scatter | solution.py:77
  25.6 2.7 copy-start.4
  30.3 1.2 copy-start.8
  30.3 1.9 copy-start.29
  30.3 2.5 slice-start
  31.6 83.3 %collective-permute-start.1 = (bf16[1024,512]{1,0:T(8,128)(2,1)S(1)}, bf16[1024,512]{1,0:T(8,128)(2,1)S(1)}, u32[]{:S(2)}, u32[]{:S(2)}) collective-permute-start(bf16[1024,512]{1,0:T(8,128)(2,1)S(1)} %bitcast.182), channel_id=1, source_target_pairs={{0,64},{64,0},{1,65},{65,1},{2,66},{66,2},{3,67},{67,3},{4,68},{68... | collective-permute-start | bytes 3145736 | tf_op jit(solution)/shard_map/ppermute | solution.py:105
  33.0 74.2 %copy-start.32 = (pred[32,32]{0,1:T(8,128)(4,1)}, pred[32,32]{0,1:T(8,128)(4,1)S(1)}, u32[]{:S(2)}) copy-start(pred[32,32]{0,1:T(8,128)(4,1)S(1)} %broadcast_compare_fusion) | copy-start | bytes 3076
  105.3 0.5 copy-start.27
  106.9 2.3 copy-start.25
  106.9 7.1 %copy-start.34 = (s32[2,16,2]{1,2,0:T(2,128)S(1)}, s32[2,16,2]{1,2,0:T(2,128)}, u32[]{:S(2)}) copy-start(s32[2,16,2]{1,2,0:T(2,128)} %param.15) | copy-start | bytes 772
  106.9 7.3 %copy-start.35 = (s32[2,16,2]{1,2,0:T(2,128)S(1)}, s32[2,16,2]{1,2,0:T(2,128)}, u32[]{:S(2)}) copy-start(s32[2,16,2]{1,2,0:T(2,128)} %param.14) | copy-start | bytes 772
  107.2 0.6 copy-start.21
  107.2 6.8 %copy-start.30 = (f32[2,4,32]{2,1,0:T(4,128)}, f32[2,4,32]{2,1,0:T(4,128)S(1)}, u32[]{:S(2)}) copy-start(f32[2,4,32]{2,1,0:T(4,128)S(1)} %get-tuple-element.26) | copy-start | bytes 3076
  109.2 19.7 %all-to-all-start.1 = ((bf16[16,32,1024]{2,1,0:T(8,128)(2,1)}), bf16[16,32,1024]{2,1,0:T(8,128)(2,1)S(1)}, u32[]{:S(2)}, u32[]{:S(2)}) async-start(bf16[16,32,1024]{2,1,0:T(8,128)(2,1)} %stack.27), calls=%async_computation.2 | async-start | bytes 2097152 | tf_op jit(solution)/shard_map/all_to_all | solution.py:82
  113.9 43.9 %reduce-scatter.9.cloned.1.call-start = ((), (), s32[]{:S(2)}) async-start(), calls=%async_computation.16 | async-start | bytes 1310720 | tf_op jit(solution)/shard_map/reduce_scatter | solution.py:77
  114.9 38.8 %copy-start.9 = (bf16[1024,512]{1,0:T(8,128)(2,1)}, bf16[1024,512]{1,0:T(8,128)(2,1)S(1)}, u32[]{:S(2)}) copy-start(bf16[1024,512]{1,0:T(8,128)(2,1)S(1)} %collective-permute-done.1) | copy-start | bytes 3145732
  128.9 27.7 %copy-start.11 = (bf16[16,32,1024]{2,1,0:T(8,128)(2,1)}, bf16[16,32,1024]{2,1,0:T(8,128)(2,1)S(1)}, u32[]{:S(2)}) copy-start(bf16[16,32,1024]{2,1,0:T(8,128)(2,1)S(1)} %all-to-all-done.1) | copy-start | bytes 3145732
  130.6 102.8 %reduce-scatter.13.cloned.1.call-start = ((), (), s32[]{:S(2)}) async-start(), calls=%async_computation.18 | async-start | bytes 2228224 | tf_op jit(solution)/shard_map/reduce_scatter | solution.py:77
  153.7 0.8 copy-start
  156.6 1.2 copy-start.19
  156.6 11.8 %copy-start.14 = (bf16[1,512,1024]{2,1,0:T(8,128)(2,1)S(1)}, bf16[1,512,1024]{2,1,0:T(8,128)(2,1)}, u32[]{:S(2)}) copy-start(bf16[1,512,1024]{2,1,0:T(8,128)(2,1)} %param.16) | copy-start | bytes 3145732
  156.6 11.8 %copy-start.17 = (bf16[1,512,256]{2,1,0:T(8,128)(2,1)S(1)}, bf16[1,512,256]{2,1,0:T(8,128)(2,1)}, u32[]{:S(2)}) copy-start(bf16[1,512,256]{2,1,0:T(8,128)(2,1)} %param.17) | copy-start | bytes 786436
  156.6 155.4 %reduce-scatter.11.cloned.1.call-start = ((), (), s32[]{:S(2)}) async-start(), calls=%async_computation.17 | async-start | bytes 3620864 | tf_op jit(solution)/shard_map/reduce_scatter | solution.py:77
  168.2 184.6 %copy-start.6 = (bf16[4,128,512]{2,1,0:T(8,128)(2,1)}, bf16[4,128,512]{2,1,0:T(8,128)(2,1)S(1)}, u32[]{:S(2)}) copy-start(bf16[4,128,512]{2,1,0:T(8,128)(2,1)S(1)} %all_to_all.46) | copy-start | bytes 1572868
  171.5 142.5 %copy-start.33 = (pred[32,32]{0,1:T(8,128)(4,1)S(1)}, pred[32,32]{0,1:T(8,128)(4,1)}, u32[]{:S(2)}) copy-start(pred[32,32]{0,1:T(8,128)(4,1)} %copy-done.32) | copy-start | bytes 3076
  312.0 3.6 copy-start.15
  314.2 1.8 copy-start.23
  329.5 23.3 %all-to-all-start.4 = ((bf16[16,32,1536]{2,1,0:T(8,128)(2,1)}), bf16[16,32,1536]{2,1,0:T(8,128)(2,1)S(1)}, u32[]{:S(2)}, u32[]{:S(2)}) async-start(bf16[16,32,1536]{2,1,0:T(8,128)(2,1)} %stack.31), calls=%async_computation.8 | async-start | bytes 3145728 | tf_op jit(solution)/shard_map/all_to_all | solution.py:82
  333.2 47.1 %reduce-scatter.15.cloned.1.call-start = ((), (), s32[]{:S(2)}) async-start(), calls=%async_computation.19 | async-start | bytes 1310720 | tf_op jit(solution)/shard_map/reduce_scatter | solution.py:77
  352.7 27.6 %copy-start.20 = (bf16[2,128,512]{2,1,0:T(8,128)(2,1)S(1)}, bf16[2,128,512]{2,1,0:T(8,128)(2,1)}, u32[]{:S(2)}) copy-start(bf16[2,128,512]{2,1,0:T(8,128)(2,1)} %param.11) | copy-start | bytes 786436
  356.2 112.9 %reduce-scatter.17.cloned.1.call-start = ((), (), s32[]{:S(2)}) async-start(), calls=%async_computation.20 | async-start | bytes 2228224 | tf_op jit(solution)/shard_map/reduce_scatter | solution.py:77
  380.3 11.3 %copy-start.10 = (bf16[1024,512]{1,0:T(8,128)(2,1)S(1)}, bf16[1024,512]{1,0:T(8,128)(2,1)}, u32[]{:S(2)}) copy-start(bf16[1024,512]{1,0:T(8,128)(2,1)} %copy-done.9) | copy-start | bytes 3145732
  390.8 0.8 copy-start.2
  393.7 76.4 %copy-start.22 = (f32[2,4,32,32]{2,3,1,0:T(8,128)S(1)}, f32[2,4,32,32]{2,3,1,0:T(8,128)}, u32[]{:S(2)}) copy-start(f32[2,4,32,32]{2,3,1,0:T(8,128)} %copy-done.21) | copy-start | bytes 98308
  393.7 76.4 %copy-start.26 = (bf16[32,2,128]{2,1,0:T(2,128)(2,1)S(1)}, bf16[32,2,128]{2,1,0:T(2,128)(2,1)}, u32[]{:S(2)}) copy-start(bf16[32,2,128]{2,1,0:T(2,128)(2,1)} %copy-done.25) | copy-start | bytes 49156
  393.7 76.4 %copy-start.31 = (f32[2,4,32]{2,1,0:T(4,128)S(1)}, f32[2,4,32]{2,1,0:T(4,128)}, u32[]{:S(2)}) copy-start(f32[2,4,32]{2,1,0:T(4,128)} %copy-done.30) | copy-start | bytes 3076
  393.7 77.7 %copy-start.28 = (f32[32]{0:T(128)S(1)}, f32[32]{0:T(128)}, u32[]{:S(2)}) copy-start(f32[32]{0:T(128)} %copy-done.27) | copy-start | bytes 388
  471.5 5.7 %copy-start.24 = (f32[2,4,32,32]{2,3,1,0:T(8,128)S(1)}, f32[2,4,32,32]{2,3,1,0:T(8,128)}, u32[]{:S(2)}) copy-start(f32[2,4,32,32]{2,3,1,0:T(8,128)} %copy-done.23) | copy-start | bytes 98308
  472.9 24.3 %all-to-all-start.7 = ((bf16[16,32,1536]{2,1,0:T(8,128)(2,1)}), bf16[16,32,1536]{2,1,0:T(8,128)(2,1)S(1)}, u32[]{:S(2)}, u32[]{:S(2)}) async-start(bf16[16,32,1536]{2,1,0:T(8,128)(2,1)} %stack.34), calls=%async_computation.13 | async-start | bytes 3145728 | tf_op jit(solution)/shard_map/all_to_all | solution.py:82
  498.2 20.3 %all-to-all-start.8 = ((bf16[16,32,1024]{2,1,0:T(8,128)(2,1)}), bf16[16,32,1024]{2,1,0:T(8,128)(2,1)}, u32[]{:S(2)}, u32[]{:S(2)}) async-start(bf16[16,32,1024]{2,1,0:T(8,128)(2,1)} %stack.35), calls=%async_computation.14 | async-start | bytes 2097152 | tf_op jit(solution)/shard_map/all_to_all | solution.py:82
  506.3 18.3 %copy-start.1 = (bf16[4,128,512]{2,1,0:T(8,128)(2,1)S(1)}, bf16[4,128,512]{2,1,0:T(8,128)(2,1)}, u32[]{:S(2)}) copy-start(bf16[4,128,512]{2,1,0:T(8,128)(2,1)} %copy-done) | copy-start | bytes 1572868
  506.3 18.3 %copy-start.3 = (bf16[4,128,512]{2,1,0:T(8,128)(2,1)S(1)}, bf16[4,128,512]{2,1,0:T(8,128)(2,1)}, u32[]{:S(2)}) copy-start(bf16[4,128,512]{2,1,0:T(8,128)(2,1)} %copy-done.2) | copy-start | bytes 1572868
  506.3 23.9 %collective-permute-start.3 = (bf16[512,1536]{1,0:T(8,128)(2,1)}, bf16[512,1536]{1,0:T(8,128)(2,1)S(1)}, u32[]{:S(2)}, u32[]{:S(2)}) collective-permute-start(bf16[512,1536]{1,0:T(8,128)(2,1)} %get-tuple-element.11), channel_id=1, source_target_pairs={{0,64},{64,0},{1,65},{65,1},{2,66},{66,2},{3,67},{67,3},{4,68},{68... | collective-permute-start | bytes 4718600 | tf_op jit(solution)/shard_map/ppermute | solution.py:170
  520.2 4.7 copy-start.5
  520.2 4.7 copy-start.7
  520.2 6.7 %collective-permute-start.4 = (bf16[512,1024]{1,0:T(8,128)(2,1)S(1)}, bf16[512,1024]{1,0:T(8,128)(2,1)S(1)}, u32[]{:S(2)}, u32[]{:S(2)}) collective-permute-start(bf16[512,1024]{1,0:T(8,128)(2,1)S(1)} %get-tuple-element.13), channel_id=1, source_target_pairs={{0,64},{64,0},{1,65},{65,1},{2,66},{66,2},{3,67},{67,3},{4,68},{68... | collective-permute-start | bytes 3145736 | tf_op jit(solution)/shard_map/ppermute | solution.py:170
  524.7 2.9 collective-permute-start.5
  525.0 5.2 collective-permute-start.2
  527.6 2.6 copy-start.12
Sparse Core Ops, SparseCore 0:
  30.5 73.9 reduce-scatter.6
  130.7 27.0 reduce-scatter.8
  162.0 71.3 reduce-scatter.12
  236.6 75.2 reduce-scatter.10
  356.3 23.9 reduce-scatter.14
  393.9 75.2 reduce-scatter.16
